TPU v7x, 256 devices: a whole 4x4x8 slice. The times are simulated.
256 devices in a mesh: inst: 32 (over z, y_lo, core), tp: 8 (over y_hi, x).
Axes of the slice: x: 4, y: 4 (y_hi: 2, y_lo: 2; y = y_hi * 2 + y_lo), z: 8, core: 2. Of those that a mesh axis runs over, the one named last changes fastest.
Arguments:
- prompt_q: bfloat16 [8192, 8192], P('inst', 'tp'), may hold values from -6 to 6
- prompt_k: bfloat16 [8192, 1024], P('inst', 'tp'), may hold values from -6 to 6
- prompt_value_rows: bfloat16 [8192, 1024], P('inst', 'tp'), may hold values from -6 to 6
- decode_q: bfloat16 [1024, 4, 8192], P('inst', None, 'tp'), may hold values from -6 to 6
- new_k: bfloat16 [1024, 4, 1024], P('inst', None, 'tp'), may hold values from -6 to 6
- new_v: bfloat16 [1024, 4, 1024], P('inst', None, 'tp'), may hold values from -6 to 6
- cache_k: bfloat16 [1024, 256, 1024], P('inst', None, 'tp'), may hold values from -6 to 6
- cache_v: bfloat16 [1024, 256, 1024], P('inst', None, 'tp'), may hold values from -6 to 6
- cache_len: int32 [1024], P('inst'), may hold values from 1 to 256, as said below
- pairing: int32 [32], replicated, may hold values from 0 to 31, each once
Outputs:
- prompt_out: bfloat16 [8192, 8192], P('inst', 'tp')
- decode_out: bfloat16 [1024, 4, 8192], P('inst', None, 'tp')
Inputs may be any that keep to these rules, and one draw needn't show every extreme that they name: `cache_len`: every instance has a row whose cache is full, at 256 live slots. `pairing`: each instance's number is named once.
All inputs are finite; a program needn't handle non-finite values.
Results may differ from a plain program's by a relative error of at most 0.006.
Values may be sent and summed in bfloat16 or wider, within the bound.
A program may use at most 64 MiB of HBM per device.

v0:
```python
import jax
import jax.numpy as jnp
from jax import lax
from jax.sharding import PartitionSpec as P

HDIM = 128


NEG = -1e30


def decode_group(dec_q, nk, nv, ck, cv, clen, pk, pv):
    rows, steps = (dec_q.shape[0], dec_q.shape[1])
    groups = nk.shape[-1] // HDIM
    ratio = dec_q.shape[-1] // (groups * HDIM)
    slots = ck.shape[1]
    plen = pk.shape[0]
    scale = HDIM ** (-0.5)
    query = dec_q.reshape(rows, steps, groups, ratio, HDIM)
    ckr = ck.reshape(rows, slots, groups, HDIM)
    cvr = cv.reshape(rows, slots, groups, HDIM)
    pkr = pk.reshape(plen, groups, HDIM)
    pvr = pv.reshape(plen, groups, HDIM)
    nkr = nk.reshape(rows, steps, groups, HDIM)
    nvr = nv.reshape(rows, steps, groups, HDIM)
    cache_keep = jnp.arange(slots, dtype=jnp.int32)[None, :] < clen[:, None]
    cache_keep = cache_keep[:, None, None, None, :]
    step_keep = (
        jnp.arange(steps, dtype=jnp.int32)[None, :] <= jnp.arange(steps, dtype=jnp.int32)[:, None]
    )
    step_keep = step_keep[None, :, None, None, :]
    s_cache = (
        jnp.einsum("asgrd,acgd->asgrc", query, ckr, preferred_element_type=jnp.float32) * scale
    )
    s_cache = jnp.where(cache_keep, s_cache, NEG)
    s_prompt = (
        jnp.einsum("asgrd,pgd->asgrp", query, pkr, preferred_element_type=jnp.float32) * scale
    )
    s_new = jnp.einsum("asgrd,atgd->asgrt", query, nkr, preferred_element_type=jnp.float32) * scale
    s_new = jnp.where(step_keep, s_new, NEG)
    top = jnp.maximum(jnp.maximum(jnp.max(s_cache, -1), jnp.max(s_prompt, -1)), jnp.max(s_new, -1))[
        ..., None
    ]
    p_cache = jnp.where(cache_keep, jnp.exp(s_cache - top), 0.0)
    p_prompt = jnp.exp(s_prompt - top)
    p_new = jnp.where(step_keep, jnp.exp(s_new - top), 0.0)
    total = jnp.sum(p_cache, -1) + jnp.sum(p_prompt, -1) + jnp.sum(p_new, -1)
    summed = jnp.einsum(
        "asgrc,acgd->asgrd", p_cache.astype(jnp.bfloat16), cvr, preferred_element_type=jnp.float32
    )
    summed = summed + jnp.einsum(
        "asgrp,pgd->asgrd", p_prompt.astype(jnp.bfloat16), pvr, preferred_element_type=jnp.float32
    )
    summed = summed + jnp.einsum(
        "asgrt,atgd->asgrd", p_new.astype(jnp.bfloat16), nvr, preferred_element_type=jnp.float32
    )
    out = summed / total[..., None]
    return out.reshape(rows, steps, groups * ratio * HDIM).astype(jnp.bfloat16)


def pick_block(held, pieces, source_row, tok_rows):
    length = pieces[0].shape[0]
    inside = jnp.logical_and(source_row >= 0, source_row < length)
    begin = jnp.clip(source_row, 0, length - tok_rows)
    taken_k = lax.dynamic_slice_in_dim(pieces[0], begin, tok_rows, 0)
    taken_v = lax.dynamic_slice_in_dim(pieces[1], begin, tok_rows, 0)
    return (jnp.where(inside, taken_k, held[0]), jnp.where(inside, taken_v, held[1]))


def per_device(
    prompt_q,
    prompt_k,
    prompt_value_rows,
    decode_q,
    new_k,
    new_v,
    cache_k,
    cache_v,
    cache_len,
    pairing,
):
    tok_rows = prompt_q.shape[0]
    groups = prompt_k.shape[1] // HDIM
    ratio = prompt_q.shape[1] // (groups * HDIM)
    scale = HDIM ** (-0.5)
    my_index = lax.axis_index("inst")
    first_row = my_index * tok_rows
    last_row = first_row + tok_rows - 1
    source_row = lax.dynamic_index_in_dim(pairing, my_index, keepdims=False) * tok_rows
    query_rows = prompt_q.reshape(tok_rows, groups, ratio, HDIM)
    query_pos = first_row + jnp.arange(tok_rows, dtype=jnp.int32)
    start_state = (
        jnp.full((groups, ratio, tok_rows), NEG, jnp.float32),
        jnp.zeros((groups, ratio, tok_rows), jnp.float32),
        jnp.zeros((groups, ratio, tok_rows, HDIM), jnp.float32),
    )
    empty = jnp.zeros(prompt_k.shape, prompt_k.dtype)
    keys = lax.all_gather(prompt_k, "inst", axis=0, tiled=True)
    values = lax.all_gather(prompt_value_rows, "inst", axis=0, tiled=True)
    length = keys.shape[0]
    width = 512

    def one_block(index, inner):
        block_start = index * width

        def update(current):
            top, total, summed = current
            key_block_rows = lax.dynamic_slice_in_dim(keys, index * width, width, 0).reshape(
                width, groups, HDIM
            )
            value_block_rows = lax.dynamic_slice_in_dim(values, index * width, width, 0).reshape(
                width, groups, HDIM
            )
            scores = (
                jnp.einsum(
                    "nfzh,ifh->fzni", query_rows, key_block_rows, preferred_element_type=jnp.float32
                )
                * scale
            )
            key_pos = block_start + jnp.arange(width, dtype=jnp.int32)
            keep = (key_pos[None, :] <= query_pos[:, None])[None, None]
            scores = jnp.where(keep, scores, NEG)
            new_top = jnp.maximum(top, jnp.max(scores, -1))
            factor = jnp.exp(top - new_top)
            attention_weights = jnp.where(keep, jnp.exp(scores - new_top[..., None]), 0.0)
            total = total * factor + jnp.sum(attention_weights, -1)
            summed = summed * factor[..., None] + jnp.einsum(
                "hylj,jhx->hylx",
                attention_weights.astype(jnp.bfloat16),
                value_block_rows,
                preferred_element_type=jnp.float32,
            )
            return (new_top, total, summed)

        return lax.cond(block_start <= last_row, update, lambda current: current, inner)

    final_state = lax.fori_loop(0, length // width, one_block, start_state)
    held = pick_block(
        (empty, empty),
        (
            lax.all_gather(prompt_k, "inst", axis=0, tiled=True),
            lax.all_gather(prompt_value_rows, "inst", axis=0, tiled=True),
        ),
        source_row,
        tok_rows,
    )
    top, total, summed = final_state
    prompt_out = (
        (summed / total[..., None])
        .transpose(2, 0, 1, 3)
        .reshape(tok_rows, groups * ratio * HDIM)
        .astype(jnp.bfloat16)
    )
    decode_out = decode_group(decode_q, new_k, new_v, cache_k, cache_v, cache_len, held[0], held[1])
    return (prompt_out, decode_out)


def solution(mesh):
    return jax.shard_map(
        per_device,
        mesh=mesh,
        in_specs=(
            P("inst", "tp"),
            P("inst", "tp"),
            P("inst", "tp"),
            P("inst", None, "tp"),
            P("inst", None, "tp"),
            P("inst", None, "tp"),
            P("inst", None, "tp"),
            P("inst", None, "tp"),
            P("inst"),
            P(),
        ),
        out_specs=(P("inst", "tp"), P("inst", None, "tp")),
        check_vma=False,
    )
```

profile of v0, /device:TPU:252, one launch (start us, length us, event | category | flops | bytes accessed | tf_op | source)
XLA Modules:
  0.0 260.8 jit_solution(9629160443537960665)
XLA Ops:
  17.8 54.8 %all-gather.3.cloned.1.call-done = bf16[8192,128]{1,0:T(8,128)(2,1)} async-done(((bf16[256,128]{1,0:T(8,128)(2,1)}), bf16[8192,128]{1,0:T(8,128)(2,1)}) %all-gather.3.cloned.1.call-update) | async-done | bytes 2097168 | tf_op jit(solution)/shard_map/all_gather | solution.py:98
  72.5 66.3 %all-gather.5.cloned.1.call-done = bf16[8192,128]{1,0:T(8,128)(2,1)} async-done(((bf16[256,128]{1,0:T(8,128)(2,1)}), bf16[8192,128]{1,0:T(8,128)(2,1)}) %all-gather.5.cloned.1.call-update) | async-done | bytes 2097168 | tf_op jit(solution)/shard_map/all_gather | solution.py:99
  139.9 105.4 %while.18 = (s32[]{:T(128)}, f32[1,8,256]{2,1,0:T(8,128)S(1)}, f32[1,8,256]{2,1,0:T(8,128)S(1)}, f32[1,8,256,128]{3,2,1,0:T(8,128)}, s32[]{:T(128)}, /*index=5*/...) while((s32[]{:T(128)}, f32[1,8,256]{2,1,0:T(8,128)S(1)}, ...), condition=%wide.region_5.6_spmd.clone, body=%wide.region_0.5_spmd.clone.sunk | while | flops 551164672 | bytes 24519052 | solution.py:137
  139.9 6.6 %conditional.3 = ((f32[1,8,256]{2,1,0:T(8,128)S(1)}, f32[1,8,256]{2,1,0:T(8,128)S(1)}, f32[1,8,256,128]{3,2,1,0:T(8,128)})) conditional(s32[]{:T(128)} %convert_element_type.68, (f32[1,8,256]{2,1,0:T(8,128)S(1)}, f32[1,8,256]{2,1,0:T(8,128)S(1)}, f32[1,8,256,128]{3,2,1,0:T(8,128)}) %tuple.53, (s32[]{:T(128)}, s32[]{:T(128)}, s32[]{:T(128)}, ...), branch_computations={%region_1.1_spmd, %region_2.4_spmd} | conditional | flops 551164672 | bytes 24517782 | solution.py:135
  143.0 2.5 fusion.12
  146.5 6.6 %conditional.3 = ((f32[1,8,256]{2,1,0:T(8,128)S(1)}, f32[1,8,256]{2,1,0:T(8,128)S(1)}, f32[1,8,256,128]{3,2,1,0:T(8,128)})) conditional(s32[]{:T(128)} %convert_element_type.68, (f32[1,8,256]{2,1,0:T(8,128)S(1)}, f32[1,8,256]{2,1,0:T(8,128)S(1)}, f32[1,8,256,128]{3,2,1,0:T(8,128)}) %tuple.53, (s32[]{:T(128)}, s32[]{:T(128)}, s32[]{:T(128)}, ...), branch_computations={%region_1.1_spmd, %region_2.4_spmd} | conditional | flops 551164672 | bytes 24517782 | solution.py:135
  149.6 2.5 fusion.12
  153.1 6.6 %conditional.3 = ((f32[1,8,256]{2,1,0:T(8,128)S(1)}, f32[1,8,256]{2,1,0:T(8,128)S(1)}, f32[1,8,256,128]{3,2,1,0:T(8,128)})) conditional(s32[]{:T(128)} %convert_element_type.68, (f32[1,8,256]{2,1,0:T(8,128)S(1)}, f32[1,8,256]{2,1,0:T(8,128)S(1)}, f32[1,8,256,128]{3,2,1,0:T(8,128)}) %tuple.53, (s32[]{:T(128)}, s32[]{:T(128)}, s32[]{:T(128)}, ...), branch_computations={%region_1.1_spmd, %region_2.4_spmd} | conditional | flops 551164672 | bytes 24517782 | solution.py:135
  156.1 2.5 fusion.12
  159.7 6.6 %conditional.3 = ((f32[1,8,256]{2,1,0:T(8,128)S(1)}, f32[1,8,256]{2,1,0:T(8,128)S(1)}, f32[1,8,256,128]{3,2,1,0:T(8,128)})) conditional(s32[]{:T(128)} %convert_element_type.68, (f32[1,8,256]{2,1,0:T(8,128)S(1)}, f32[1,8,256]{2,1,0:T(8,128)S(1)}, f32[1,8,256,128]{3,2,1,0:T(8,128)}) %tuple.53, (s32[]{:T(128)}, s32[]{:T(128)}, s32[]{:T(128)}, ...), branch_computations={%region_1.1_spmd, %region_2.4_spmd} | conditional | flops 551164672 | bytes 24517782 | solution.py:135
  162.7 2.5 fusion.12
  166.3 6.6 %conditional.3 = ((f32[1,8,256]{2,1,0:T(8,128)S(1)}, f32[1,8,256]{2,1,0:T(8,128)S(1)}, f32[1,8,256,128]{3,2,1,0:T(8,128)})) conditional(s32[]{:T(128)} %convert_element_type.68, (f32[1,8,256]{2,1,0:T(8,128)S(1)}, f32[1,8,256]{2,1,0:T(8,128)S(1)}, f32[1,8,256,128]{3,2,1,0:T(8,128)}) %tuple.53, (s32[]{:T(128)}, s32[]{:T(128)}, s32[]{:T(128)}, ...), branch_computations={%region_1.1_spmd, %region_2.4_spmd} | conditional | flops 551164672 | bytes 24517782 | solution.py:135
  169.3 2.5 fusion.12
  172.9 6.6 %conditional.3 = ((f32[1,8,256]{2,1,0:T(8,128)S(1)}, f32[1,8,256]{2,1,0:T(8,128)S(1)}, f32[1,8,256,128]{3,2,1,0:T(8,128)})) conditional(s32[]{:T(128)} %convert_element_type.68, (f32[1,8,256]{2,1,0:T(8,128)S(1)}, f32[1,8,256]{2,1,0:T(8,128)S(1)}, f32[1,8,256,128]{3,2,1,0:T(8,128)}) %tuple.53, (s32[]{:T(128)}, s32[]{:T(128)}, s32[]{:T(128)}, ...), branch_computations={%region_1.1_spmd, %region_2.4_spmd} | conditional | flops 551164672 | bytes 24517782 | solution.py:135
  179.4 6.6 %conditional.3 = ((f32[1,8,256]{2,1,0:T(8,128)S(1)}, f32[1,8,256]{2,1,0:T(8,128)S(1)}, f32[1,8,256,128]{3,2,1,0:T(8,128)})) conditional(s32[]{:T(128)} %convert_element_type.68, (f32[1,8,256]{2,1,0:T(8,128)S(1)}, f32[1,8,256]{2,1,0:T(8,128)S(1)}, f32[1,8,256,128]{3,2,1,0:T(8,128)}) %tuple.53, (s32[]{:T(128)}, s32[]{:T(128)}, s32[]{:T(128)}, ...), branch_computations={%region_1.1_spmd, %region_2.4_spmd} | conditional | flops 551164672 | bytes 24517782 | solution.py:135
  182.5 2.5 fusion.12
  186.0 6.6 %conditional.3 = ((f32[1,8,256]{2,1,0:T(8,128)S(1)}, f32[1,8,256]{2,1,0:T(8,128)S(1)}, f32[1,8,256,128]{3,2,1,0:T(8,128)})) conditional(s32[]{:T(128)} %convert_element_type.68, (f32[1,8,256]{2,1,0:T(8,128)S(1)}, f32[1,8,256]{2,1,0:T(8,128)S(1)}, f32[1,8,256,128]{3,2,1,0:T(8,128)}) %tuple.53, (s32[]{:T(128)}, s32[]{:T(128)}, s32[]{:T(128)}, ...), branch_computations={%region_1.1_spmd, %region_2.4_spmd} | conditional | flops 551164672 | bytes 24517782 | solution.py:135
  189.1 2.5 fusion.12
  192.6 6.6 %conditional.3 = ((f32[1,8,256]{2,1,0:T(8,128)S(1)}, f32[1,8,256]{2,1,0:T(8,128)S(1)}, f32[1,8,256,128]{3,2,1,0:T(8,128)})) conditional(s32[]{:T(128)} %convert_element_type.68, (f32[1,8,256]{2,1,0:T(8,128)S(1)}, f32[1,8,256]{2,1,0:T(8,128)S(1)}, f32[1,8,256,128]{3,2,1,0:T(8,128)}) %tuple.53, (s32[]{:T(128)}, s32[]{:T(128)}, s32[]{:T(128)}, ...), branch_computations={%region_1.1_spmd, %region_2.4_spmd} | conditional | flops 551164672 | bytes 24517782 | solution.py:135
  195.7 2.5 fusion.12
  199.2 6.6 %conditional.3 = ((f32[1,8,256]{2,1,0:T(8,128)S(1)}, f32[1,8,256]{2,1,0:T(8,128)S(1)}, f32[1,8,256,128]{3,2,1,0:T(8,128)})) conditional(s32[]{:T(128)} %convert_element_type.68, (f32[1,8,256]{2,1,0:T(8,128)S(1)}, f32[1,8,256]{2,1,0:T(8,128)S(1)}, f32[1,8,256,128]{3,2,1,0:T(8,128)}) %tuple.53, (s32[]{:T(128)}, s32[]{:T(128)}, s32[]{:T(128)}, ...), branch_computations={%region_1.1_spmd, %region_2.4_spmd} | conditional | flops 551164672 | bytes 24517782 | solution.py:135
  202.2 2.5 fusion.12
  205.8 6.6 %conditional.3 = ((f32[1,8,256]{2,1,0:T(8,128)S(1)}, f32[1,8,256]{2,1,0:T(8,128)S(1)}, f32[1,8,256,128]{3,2,1,0:T(8,128)})) conditional(s32[]{:T(128)} %convert_element_type.68, (f32[1,8,256]{2,1,0:T(8,128)S(1)}, f32[1,8,256]{2,1,0:T(8,128)S(1)}, f32[1,8,256,128]{3,2,1,0:T(8,128)}) %tuple.53, (s32[]{:T(128)}, s32[]{:T(128)}, s32[]{:T(128)}, ...), branch_computations={%region_1.1_spmd, %region_2.4_spmd} | conditional | flops 551164672 | bytes 24517782 | solution.py:135
  208.8 2.5 fusion.12
  212.4 6.6 %conditional.3 = ((f32[1,8,256]{2,1,0:T(8,128)S(1)}, f32[1,8,256]{2,1,0:T(8,128)S(1)}, f32[1,8,256,128]{3,2,1,0:T(8,128)})) conditional(s32[]{:T(128)} %convert_element_type.68, (f32[1,8,256]{2,1,0:T(8,128)S(1)}, f32[1,8,256]{2,1,0:T(8,128)S(1)}, f32[1,8,256,128]{3,2,1,0:T(8,128)}) %tuple.53, (s32[]{:T(128)}, s32[]{:T(128)}, s32[]{:T(128)}, ...), branch_computations={%region_1.1_spmd, %region_2.4_spmd} | conditional | flops 551164672 | bytes 24517782 | solution.py:135
  215.4 2.5 fusion.12
  219.0 6.6 %conditional.3 = ((f32[1,8,256]{2,1,0:T(8,128)S(1)}, f32[1,8,256]{2,1,0:T(8,128)S(1)}, f32[1,8,256,128]{3,2,1,0:T(8,128)})) conditional(s32[]{:T(128)} %convert_element_type.68, (f32[1,8,256]{2,1,0:T(8,128)S(1)}, f32[1,8,256]{2,1,0:T(8,128)S(1)}, f32[1,8,256,128]{3,2,1,0:T(8,128)}) %tuple.53, (s32[]{:T(128)}, s32[]{:T(128)}, s32[]{:T(128)}, ...), branch_computations={%region_1.1_spmd, %region_2.4_spmd} | conditional | flops 551164672 | bytes 24517782 | solution.py:135
  222.0 2.5 fusion.12
  225.5 6.6 %conditional.3 = ((f32[1,8,256]{2,1,0:T(8,128)S(1)}, f32[1,8,256]{2,1,0:T(8,128)S(1)}, f32[1,8,256,128]{3,2,1,0:T(8,128)})) conditional(s32[]{:T(128)} %convert_element_type.68, (f32[1,8,256]{2,1,0:T(8,128)S(1)}, f32[1,8,256]{2,1,0:T(8,128)S(1)}, f32[1,8,256,128]{3,2,1,0:T(8,128)}) %tuple.53, (s32[]{:T(128)}, s32[]{:T(128)}, s32[]{:T(128)}, ...), branch_computations={%region_1.1_spmd, %region_2.4_spmd} | conditional | flops 551164672 | bytes 24517782 | solution.py:135
  228.6 2.5 fusion.12
  232.1 6.6 %conditional.3 = ((f32[1,8,256]{2,1,0:T(8,128)S(1)}, f32[1,8,256]{2,1,0:T(8,128)S(1)}, f32[1,8,256,128]{3,2,1,0:T(8,128)})) conditional(s32[]{:T(128)} %convert_element_type.68, (f32[1,8,256]{2,1,0:T(8,128)S(1)}, f32[1,8,256]{2,1,0:T(8,128)S(1)}, f32[1,8,256,128]{3,2,1,0:T(8,128)}) %tuple.53, (s32[]{:T(128)}, s32[]{:T(128)}, s32[]{:T(128)}, ...), branch_computations={%region_1.1_spmd, %region_2.4_spmd} | conditional | flops 551164672 | bytes 24517782 | solution.py:135
  238.7 6.6 %conditional.3 = ((f32[1,8,256]{2,1,0:T(8,128)S(1)}, f32[1,8,256]{2,1,0:T(8,128)S(1)}, f32[1,8,256,128]{3,2,1,0:T(8,128)})) conditional(s32[]{:T(128)} %convert_element_type.68, (f32[1,8,256]{2,1,0:T(8,128)S(1)}, f32[1,8,256]{2,1,0:T(8,128)S(1)}, f32[1,8,256,128]{3,2,1,0:T(8,128)}) %tuple.53, (s32[]{:T(128)}, s32[]{:T(128)}, s32[]{:T(128)}, ...), branch_computations={%region_1.1_spmd, %region_2.4_spmd} | conditional | flops 551164672 | bytes 24517782 | solution.py:135
  (246 shorter events, 90.8 us)
Async XLA Ops:
  7.2 8.8 %copy-start = (bf16[32,256,128]{2,1,0:T(8,128)(2,1)S(1)}, bf16[32,256,128]{2,1,0:T(8,128)(2,1)}, u32[]{:S(2)}) copy-start(bf16[32,256,128]{2,1,0:T(8,128)(2,1)} %param.20) | copy-start | bytes 6291460
  7.2 65.4 %all-gather.3.cloned.1.call-start = ((), (), s32[]{:S(2)}) async-start(), calls=%async_computation | async-start | bytes 2162688 | tf_op jit(solution)/shard_map/all_gather | solution.py:98
  7.9 130.9 %all-gather.5.cloned.1.call-start = ((), (), s32[]{:S(2)}) async-start(), calls=%async_computation.1 | async-start | bytes 2162688 | tf_op jit(solution)/shard_map/all_gather | solution.py:99
  140.1 2.9 %copy-start.2 = (f32[1,8,256,128]{3,2,1,0:T(8,128)S(1)}, f32[1,8,256,128]{3,2,1,0:T(8,128)}, u32[]{:S(2)}) copy-start(f32[1,8,256,128]{3,2,1,0:T(8,128)} %get-tuple-element.180) | copy-start | bytes 3145732 | tf_op jit(solution)/shard_map/while/body/eval_jaxpr/cond
  145.5 1.0 copy-start.3
  146.7 2.9 %copy-start.2 = (f32[1,8,256,128]{3,2,1,0:T(8,128)S(1)}, f32[1,8,256,128]{3,2,1,0:T(8,128)}, u32[]{:S(2)}) copy-start(f32[1,8,256,128]{3,2,1,0:T(8,128)} %get-tuple-element.180) | copy-start | bytes 3145732 | tf_op jit(solution)/shard_map/while/body/eval_jaxpr/cond
  152.1 1.0 copy-start.3
  153.3 2.9 %copy-start.2 = (f32[1,8,256,128]{3,2,1,0:T(8,128)S(1)}, f32[1,8,256,128]{3,2,1,0:T(8,128)}, u32[]{:S(2)}) copy-start(f32[1,8,256,128]{3,2,1,0:T(8,128)} %get-tuple-element.180) | copy-start | bytes 3145732 | tf_op jit(solution)/shard_map/while/body/eval_jaxpr/cond
  158.7 1.0 copy-start.3
  159.9 2.9 %copy-start.2 = (f32[1,8,256,128]{3,2,1,0:T(8,128)S(1)}, f32[1,8,256,128]{3,2,1,0:T(8,128)}, u32[]{:S(2)}) copy-start(f32[1,8,256,128]{3,2,1,0:T(8,128)} %get-tuple-element.180) | copy-start | bytes 3145732 | tf_op jit(solution)/shard_map/while/body/eval_jaxpr/cond
  165.3 1.0 copy-start.3
  166.4 2.9 %copy-start.2 = (f32[1,8,256,128]{3,2,1,0:T(8,128)S(1)}, f32[1,8,256,128]{3,2,1,0:T(8,128)}, u32[]{:S(2)}) copy-start(f32[1,8,256,128]{3,2,1,0:T(8,128)} %get-tuple-element.180) | copy-start | bytes 3145732 | tf_op jit(solution)/shard_map/while/body/eval_jaxpr/cond
  173.0 2.9 %copy-start.2 = (f32[1,8,256,128]{3,2,1,0:T(8,128)S(1)}, f32[1,8,256,128]{3,2,1,0:T(8,128)}, u32[]{:S(2)}) copy-start(f32[1,8,256,128]{3,2,1,0:T(8,128)} %get-tuple-element.180) | copy-start | bytes 3145732 | tf_op jit(solution)/shard_map/while/body/eval_jaxpr/cond
  179.6 2.9 %copy-start.2 = (f32[1,8,256,128]{3,2,1,0:T(8,128)S(1)}, f32[1,8,256,128]{3,2,1,0:T(8,128)}, u32[]{:S(2)}) copy-start(f32[1,8,256,128]{3,2,1,0:T(8,128)} %get-tuple-element.180) | copy-start | bytes 3145732 | tf_op jit(solution)/shard_map/while/body/eval_jaxpr/cond
  186.2 2.9 %copy-start.2 = (f32[1,8,256,128]{3,2,1,0:T(8,128)S(1)}, f32[1,8,256,128]{3,2,1,0:T(8,128)}, u32[]{:S(2)}) copy-start(f32[1,8,256,128]{3,2,1,0:T(8,128)} %get-tuple-element.180) | copy-start | bytes 3145732 | tf_op jit(solution)/shard_map/while/body/eval_jaxpr/cond
  191.6 1.0 copy-start.3
  192.8 2.9 %copy-start.2 = (f32[1,8,256,128]{3,2,1,0:T(8,128)S(1)}, f32[1,8,256,128]{3,2,1,0:T(8,128)}, u32[]{:S(2)}) copy-start(f32[1,8,256,128]{3,2,1,0:T(8,128)} %get-tuple-element.180) | copy-start | bytes 3145732 | tf_op jit(solution)/shard_map/while/body/eval_jaxpr/cond
  198.2 1.0 copy-start.3
  199.4 2.9 %copy-start.2 = (f32[1,8,256,128]{3,2,1,0:T(8,128)S(1)}, f32[1,8,256,128]{3,2,1,0:T(8,128)}, u32[]{:S(2)}) copy-start(f32[1,8,256,128]{3,2,1,0:T(8,128)} %get-tuple-element.180) | copy-start | bytes 3145732 | tf_op jit(solution)/shard_map/while/body/eval_jaxpr/cond
  204.8 1.0 copy-start.3
  206.0 2.9 %copy-start.2 = (f32[1,8,256,128]{3,2,1,0:T(8,128)S(1)}, f32[1,8,256,128]{3,2,1,0:T(8,128)}, u32[]{:S(2)}) copy-start(f32[1,8,256,128]{3,2,1,0:T(8,128)} %get-tuple-element.180) | copy-start | bytes 3145732 | tf_op jit(solution)/shard_map/while/body/eval_jaxpr/cond
  212.5 2.9 %copy-start.2 = (f32[1,8,256,128]{3,2,1,0:T(8,128)S(1)}, f32[1,8,256,128]{3,2,1,0:T(8,128)}, u32[]{:S(2)}) copy-start(f32[1,8,256,128]{3,2,1,0:T(8,128)} %get-tuple-element.180) | copy-start | bytes 3145732 | tf_op jit(solution)/shard_map/while/body/eval_jaxpr/cond
  219.1 2.9 %copy-start.2 = (f32[1,8,256,128]{3,2,1,0:T(8,128)S(1)}, f32[1,8,256,128]{3,2,1,0:T(8,128)}, u32[]{:S(2)}) copy-start(f32[1,8,256,128]{3,2,1,0:T(8,128)} %get-tuple-element.180) | copy-start | bytes 3145732 | tf_op jit(solution)/shard_map/while/body/eval_jaxpr/cond
  225.7 2.9 %copy-start.2 = (f32[1,8,256,128]{3,2,1,0:T(8,128)S(1)}, f32[1,8,256,128]{3,2,1,0:T(8,128)}, u32[]{:S(2)}) copy-start(f32[1,8,256,128]{3,2,1,0:T(8,128)} %get-tuple-element.180) | copy-start | bytes 3145732 | tf_op jit(solution)/shard_map/while/body/eval_jaxpr/cond
  231.1 1.0 copy-start.3
  232.3 2.9 %copy-start.2 = (f32[1,8,256,128]{3,2,1,0:T(8,128)S(1)}, f32[1,8,256,128]{3,2,1,0:T(8,128)}, u32[]{:S(2)}) copy-start(f32[1,8,256,128]{3,2,1,0:T(8,128)} %get-tuple-element.180) | copy-start | bytes 3145732 | tf_op jit(solution)/shard_map/while/body/eval_jaxpr/cond
  237.7 1.0 copy-start.3
  238.9 2.9 %copy-start.2 = (f32[1,8,256,128]{3,2,1,0:T(8,128)S(1)}, f32[1,8,256,128]{3,2,1,0:T(8,128)}, u32[]{:S(2)}) copy-start(f32[1,8,256,128]{3,2,1,0:T(8,128)} %get-tuple-element.180) | copy-start | bytes 3145732 | tf_op jit(solution)/shard_map/while/body/eval_jaxpr/cond
  244.3 1.0 copy-start.3
  245.3 4.6 %copy-start.5 = (bf16[32,4,128]{2,1,0:T(4,128)(2,1)S(1)}, bf16[32,4,128]{2,1,0:T(4,128)(2,1)}, u32[]{:S(2)}) copy-start(bf16[32,4,128]{2,1,0:T(4,128)(2,1)} %param.19) | copy-start | bytes 98308
  245.3 4.9 %copy-start.1 = (f32[32,4,1,8,256]{4,3,1,0,2:T(8,128)S(1)}, f32[32,4,1,8,256]{4,3,1,0,2:T(8,128)}, u32[]{:S(2)}) copy-start(f32[32,4,1,8,256]{4,3,1,0,2:T(8,128)} %get-tuple-element.264) | copy-start | bytes 3145732
  245.3 4.9 %copy-start.4 = (bf16[32,256,128]{2,1,0:T(8,128)(2,1)S(1)}, bf16[32,256,128]{2,1,0:T(8,128)(2,1)}, u32[]{:S(2)}) copy-start(bf16[32,256,128]{2,1,0:T(8,128)(2,1)} %param.21) | copy-start | bytes 6291460
  (6 other events, 6.1 us)
Sparse Core Ops, SparseCore 0:
  9.9 62.6 all-gather.2
  74.4 64.3 all-gather.4
where the time goes:
time: 262 us; the launch traced here: 261 us
  waiting for transfers between devices  122 us (47%)
  matrix products  76 us (29%)
  local copies, waits for them, and re-layouts  23.3 us (9%)
  other arithmetic  22.8 us (9%)
  between operations  14.8 us (6%)
    all_gather x1, waiting for transfers between devices, per_device(): values = lax.all_gather(prompt_value_rows, 'inst', axis=0, tiled=True)  66.3 us
    all_gather x1, waiting for transfers between devices, per_device(): keys = lax.all_gather(prompt_k, 'inst', axis=0, tiled=True)  54.8 us
    dot_general x16, matrix products, update(): jnp.einsum('hylj,jhx->hylx', attention_weights.astype(jnp.bfloat16), valu...  40.4 us
    dot_general x16, matrix products, update(): jnp.einsum('nfzh,ifh->fzni', query_rows, key_block_rows, preferred_elemen...  28.4 us
    cond x80, local copies, waits for them, and re-layouts  16.3 us
    reduce_sum x16, other arithmetic, update(): total = total * factor + jnp.sum(attention_weights, -1)  16.2 us
  transfers between devices with their start and end apart: 2, of which 2 were waited for; matrix products, arithmetic and copies ran while one was open for 3% of the time, Pallas kernels for 0%

commit v1 on v0

v1 whole, which is shorter than its diff:
```python
import math

import jax
import jax.numpy as jnp
from jax import lax
from jax.experimental import pallas as pl
from jax.experimental.pallas import tpu as pltpu
from jax.sharding import PartitionSpec as P

MESH = pl.DeviceIdType.MESH
BF16 = jnp.bfloat16
F32 = jnp.float32

HDIM = 128
HEADS = 8
TOK = 256
ROWS = 32
CACHE = 256
STEPS = 4
NZ = 8
NINST = 32
CELL = 4 * TOK
NEG = -1e30
FACTOR = HDIM**-0.5 * math.log2(math.e)

ROUTE = {}
for _d in (1, 2, 3):
    for _part in (0, 1):
        ROUTE["A", -_d, _part] = "down"
        ROUTE["A", _d, _part] = "up"
    ROUTE["B", -_d, 0] = "down"
    ROUTE["B", _d, 1] = "up"
    ROUTE["B", _d, 0] = "side"
    ROUTE["B", -_d, 1] = "side"
ROUTE["A", -4, 0] = "down"
ROUTE["A", 4, 1] = "up"
ROUTE["B", 0, 0] = "side"
ROUTE["B", 0, 1] = "side"
ROUTE["B", -4, 0] = "side"
ROUTE["B", 4, 1] = "side"

EVENTS_NEAR = [("A", -1, 0), ("A", 1, 0), ("A", -1, 1), ("A", 1, 1)]
EVENTS_SIDE = [("B", 0, 0), ("B", 0, 1)]
EVENTS_OWN = [
    ("B", 1, 0),
    ("A", -2, 0),
    ("A", 2, 0),
    ("A", -2, 1),
    ("A", 2, 1),
    ("B", -1, 1),
]
EVENTS_LOOP = [
    [("B", -1, 0), ("B", 1, 1)],
    [("B", 2, 0), ("B", -2, 1)],
    [("A", -3, 0), ("A", 3, 1), ("A", -3, 1), ("A", 3, 0)],
    [("B", -2, 0), ("B", 2, 1)],
    [("B", 3, 0), ("B", -3, 1), ("A", -4, 0), ("A", 4, 1)],
    [("B", -3, 0), ("B", 3, 1)],
    [("B", -4, 0), ("B", 4, 1)],
]
CELL_ORDER = (-1, 1, -2, 2, -3, 3, 4)


def forwards(item):
    col, d, part = item
    to = []
    if ROUTE.get((col, d - 1, part)) == "down":
        to.append("up")
    if ROUTE.get((col, d + 1, part)) == "up":
        to.append("down")
    if col == "A" and ROUTE.get(("B", d, part)) == "side":
        to.append("side")
    to.append("twin")
    return to


OWN = [("A", 0, 0), ("A", 0, 1)]
SENDS = [(item, to) for item in OWN + list(ROUTE) for to in forwards(item)]
SEND_INDEX = {key: i for i, key in enumerate(SENDS)}


def kernel(
    q_hbm, k_hbm, v_hbm, dq_hbm, nk_hbm, nv_hbm, ck_hbm, cv_hbm, clen_ref, pair_ref,
    o_hbm, do_hbm,
    kv, q, dq, nk, nv, ck, cv, qs, acc, top, vd, dqf, dqs, dacc, dtop, nkf, nvf, out, dout,
    send_sem, recv_sem, local_sem, cache_sem,
):
    me = lax.axis_index("inst")
    core = lax.rem(me, 2)
    y = lax.rem(me // 2, 2)
    z = me // 4

    def slot(col, d):
        zz = lax.rem(z + (d + NZ), NZ)
        yy = y if col == "A" else 1 - y
        return 4 * zz + 2 * yy + core

    device = {
        "up": 4 * lax.rem(z + 1, NZ) + 2 * y + core,
        "down": 4 * lax.rem(z + NZ - 1, NZ) + 2 * y + core,
        "side": 4 * z + 2 * (1 - y) + core,
        "twin": 4 * z + 2 * y + 1 - core,
    }

    def remote(item, to):
        col, d, part = item
        place = slot(col, d)
        return pltpu.make_async_remote_copy(
            src_ref=kv.at[place, part],
            dst_ref=kv.at[place, part],
            send_sem=send_sem.at[SEND_INDEX[item, to]],
            recv_sem=recv_sem.at[place, part],
            device_id={"inst": device[to]},
            device_id_type=MESH,
        )

    def arrived(place, part):
        pltpu.make_async_remote_copy(
            src_ref=kv.at[place, part],
            dst_ref=kv.at[place, part],
            send_sem=send_sem.at[0],
            recv_sem=recv_sem.at[place, part],
            device_id={"inst": device["twin"]},
            device_id_type=MESH,
        ).wait_recv()

    def events(items):
        for item in items:
            arrived(slot(item[0], item[1]), item[2])
            for to in forwards(item):
                remote(item, to).start()

    def twin_cell(zz):
        for yy in (0, 1):
            place = 4 * zz + 2 * yy + 1 - core
            arrived(place, 0)
            arrived(place, 1)

    own = [
        pltpu.make_async_copy(k_hbm, kv.at[me, 0], local_sem.at[0]),
        pltpu.make_async_copy(v_hbm, kv.at[me, 1], local_sem.at[1]),
    ]
    small = [
        pltpu.make_async_copy(dq_hbm, dq, local_sem.at[2]),
        pltpu.make_async_copy(nk_hbm, nk, local_sem.at[3]),
        pltpu.make_async_copy(nv_hbm, nv, local_sem.at[4]),
    ]
    queries = pltpu.make_async_copy(q_hbm, q, local_sem.at[5])

    def cache_copies(g):
        rows = pl.ds(8 * g, 8)
        return (
            pltpu.make_async_copy(ck_hbm.at[rows], ck.at[rows], cache_sem.at[g, 0]),
            pltpu.make_async_copy(cv_hbm.at[rows], cv.at[rows], cache_sem.at[g, 1]),
        )

    for copy in own + small:
        copy.start()
    for g in range(4):
        for copy in cache_copies(g):
            copy.start()
    queries.start()

    barrier = pltpu.get_barrier_semaphore()
    for to in ("up", "down", "side", "twin"):
        pl.semaphore_signal(barrier, inc=1, device_id={"inst": device[to]}, device_id_type=MESH)
    pl.semaphore_wait(barrier, 4)

    for part in (0, 1):
        own[part].wait()
        for to in forwards(OWN[part]):
            remote(OWN[part], to).start()

    for copy in small:
        copy.wait()
    for h in range(HEADS):
        dqf[:, pl.ds(h, STEPS, stride=HEADS), :] = dq[:, :, h * HDIM : (h + 1) * HDIM].astype(F32)
    dqs[...] = dqf[...].astype(BF16)
    for a in range(ROWS):
        nkf[a * STEPS : (a + 1) * STEPS, :] = nk[a].astype(F32)
        nvf[a * STEPS : (a + 1) * STEPS, :] = nv[a].astype(F32)
    vd[:, HDIM:] = jnp.ones((CELL, HDIM), BF16)

    def dot_t(a, b):
        return lax.dot_general(a, b, (((1,), (1,)), ((), ())), preferred_element_type=F32)

    def wide(x, width):
        return jnp.concatenate([x] * (width // HDIM), axis=1)

    ones = jnp.ones((CACHE, HDIM), BF16)

    def decode_rows(g):
        for copy in cache_copies(g):
            copy.wait()
        for u in range(8):
            a = 8 * g + u
            scores = dot_t(dqs[a], ck[a]) * FACTOR
            live = lax.broadcasted_iota(jnp.int32, scores.shape, 1) < clen_ref[a]
            scores = jnp.where(live, scores, NEG)
            peak = jnp.max(scores, axis=1, keepdims=True)
            p = jnp.exp2(scores - peak).astype(BF16)
            dtop[a] = jnp.broadcast_to(peak, (STEPS * HEADS, HDIM))
            dacc[a] = jnp.dot(
                p, jnp.concatenate([cv[a], ones], axis=1), preferred_element_type=F32
            )

    def decode_pair(g, _):
        decode_rows(g)
        return 0

    lax.fori_loop(0, 2, decode_pair, 0)
    events(EVENTS_NEAR)
    lax.fori_loop(2, 4, decode_pair, 0)
    events(EVENTS_SIDE)

    queries.wait()
    for h in range(HEADS):
        qs[h] = q[:, h * HDIM : (h + 1) * HDIM]
    twin_cell(z)

    def cell_keys(zz):
        return kv[pl.ds(4 * zz, 4), 0].reshape(CELL, HDIM)

    def load_values(zz):
        vd[:, :HDIM] = kv[pl.ds(4 * zz, 4), 1].reshape(CELL, HDIM)

    load_values(z)

    def first_cell(half):
        for u in range(HEADS // 2):
            h = half * (HEADS // 2) + u
            scores = dot_t(qs[h], cell_keys(z)) * FACTOR
            key = lax.broadcasted_iota(jnp.int32, scores.shape, 1)
            row = lax.broadcasted_iota(jnp.int32, scores.shape, 0)
            scores = jnp.where(key <= row + TOK * lax.rem(me, 4), scores, NEG)
            peak = jnp.max(scores, axis=1, keepdims=True)
            p = jnp.exp2(scores - peak).astype(BF16)
            top[h] = jnp.broadcast_to(peak, (TOK, HDIM))
            acc[h] = jnp.dot(p, vd[...], preferred_element_type=F32)

    def first_half(half, _):
        first_cell(half)

        @pl.when(half == 0)
        def _():
            events(EVENTS_OWN)

        return 0

    lax.fori_loop(0, 2, first_half, 0)

    def merge(scores, values, top_ref, acc_ref, index):
        before = top_ref[index]
        peak = jnp.maximum(before, jnp.max(scores, axis=1, keepdims=True))
        top_ref[index] = peak
        p = jnp.exp2(scores - wide(peak, scores.shape[1])).astype(BF16)
        scale = jnp.exp2(before - peak)
        return wide(scale, 2 * HDIM) * acc_ref[index] + jnp.dot(
            p, values, preferred_element_type=F32
        )

    def cell_step(t, _):
        half = lax.rem(t, 2)
        j = t // 2
        for i, items in enumerate(EVENTS_LOOP):

            @pl.when(t == i)
            def _(items=items):
                events(items)

        away = j // 2 + 1
        zz = lax.rem(z + NZ + jnp.where(lax.rem(j, 2) == 0, -away, away), NZ)

        @pl.when(half == 0)
        def _():
            twin_cell(zz)

        @pl.when(zz < z)
        def _():
            @pl.when(half == 0)
            def _():
                load_values(zz)

            for u in range(HEADS // 2):
                h = half * (HEADS // 2) + u
                scores = dot_t(qs[h], cell_keys(zz)) * FACTOR
                acc[h] = merge(scores, vd[...], top, acc, h)

        return 0

    lax.fori_loop(0, 14, cell_step, 0)

    for h in range(HEADS):
        out[:, h * HDIM : (h + 1) * HDIM] = (acc[h, :, :HDIM] / acc[h, :, HDIM:]).astype(BF16)
    out_copy = pltpu.make_async_copy(out, o_hbm, local_sem.at[6])
    out_copy.start()

    pair = pair_ref[me]
    new_keys = ROWS * STEPS
    keys = jnp.concatenate([kv[pair, 0], nkf[...].astype(BF16)], axis=0)
    vd[:TOK, :HDIM] = kv[pair, 1]
    vd[TOK : TOK + new_keys, :HDIM] = nvf[...].astype(BF16)
    values = vd[: TOK + new_keys, :]
    per = STEPS * HEADS

    def decode_last(g, _):
        rows = pl.ds(8 * g, 8)
        size = 8 * per
        scores = dot_t(dqs[rows].reshape(size, HDIM), keys) * FACTOR
        column = lax.broadcasted_iota(jnp.int32, (size, new_keys), 1)
        row = lax.broadcasted_iota(jnp.int32, (size, new_keys), 0) + g * size
        keep = jnp.logical_and(
            column // STEPS == row // per,
            lax.rem(column, STEPS) <= lax.rem(row // HEADS, STEPS),
        )
        fresh = jnp.where(keep, scores[:, TOK:], NEG)
        scores = jnp.concatenate([scores[:, :TOK], fresh], axis=1)
        before = dtop[rows].reshape(size, HDIM)
        peak = jnp.maximum(before, jnp.max(scores, axis=1, keepdims=True))
        p = jnp.exp2(scores - wide(peak, TOK + new_keys)).astype(BF16)
        total = wide(jnp.exp2(before - peak), 2 * HDIM) * dacc[rows].reshape(size, 2 * HDIM)
        total = total + jnp.dot(p, values, preferred_element_type=F32)
        dqf[rows] = (total[:, :HDIM] / total[:, HDIM:]).reshape(8, per, HDIM)
        return 0

    lax.fori_loop(0, 4, decode_last, 0)
    for h in range(HEADS):
        dout[:, :, h * HDIM : (h + 1) * HDIM] = dqf[:, pl.ds(h, STEPS, stride=HEADS), :].astype(BF16)
    dout_copy = pltpu.make_async_copy(dout, do_hbm, local_sem.at[7])
    dout_copy.start()
    for item, to in SENDS:
        remote(item, to).wait_send()
    out_copy.wait()
    dout_copy.wait()


def per_device(*args):
    any_spec = pl.BlockSpec(memory_space=pl.ANY)
    smem = pl.BlockSpec(memory_space=pltpu.SMEM)
    vmem = pltpu.VMEM
    per = STEPS * HEADS
    return pl.pallas_call(
        kernel,
        out_shape=(
            jax.ShapeDtypeStruct((TOK, HEADS * HDIM), BF16),
            jax.ShapeDtypeStruct((ROWS, STEPS, HEADS * HDIM), BF16),
        ),
        in_specs=[any_spec] * 8 + [smem, smem],
        out_specs=(any_spec, any_spec),
        scratch_shapes=[
            vmem((NINST, 2, TOK, HDIM), BF16),
            vmem((TOK, HEADS * HDIM), BF16),
            vmem((ROWS, STEPS, HEADS * HDIM), BF16),
            vmem((ROWS, STEPS, HDIM), BF16),
            vmem((ROWS, STEPS, HDIM), BF16),
            vmem((ROWS, CACHE, HDIM), BF16),
            vmem((ROWS, CACHE, HDIM), BF16),
            vmem((HEADS, TOK, HDIM), BF16),
            vmem((HEADS, TOK, 2 * HDIM), F32),
            vmem((HEADS, TOK, HDIM), F32),
            vmem((CELL, 2 * HDIM), BF16),
            vmem((ROWS, per, HDIM), F32),
            vmem((ROWS, per, HDIM), BF16),
            vmem((ROWS, per, 2 * HDIM), F32),
            vmem((ROWS, per, HDIM), F32),
            vmem((ROWS * STEPS, HDIM), F32),
            vmem((ROWS * STEPS, HDIM), F32),
            vmem((TOK, HEADS * HDIM), BF16),
            vmem((ROWS, STEPS, HEADS * HDIM), BF16),
            pltpu.SemaphoreType.DMA((len(SENDS),)),
            pltpu.SemaphoreType.DMA((NINST, 2)),
            pltpu.SemaphoreType.DMA((8,)),
            pltpu.SemaphoreType.DMA((4, 2)),
        ],
        compiler_params=pltpu.CompilerParams(
            collective_id=0, has_side_effects=True, vmem_limit_bytes=56 * 2**20
        ),
    )(*args)


def solution(mesh):
    return jax.shard_map(
        per_device,
        mesh=mesh,
        in_specs=(
            P("inst", "tp"),
            P("inst", "tp"),
            P("inst", "tp"),
            P("inst", None, "tp"),
            P("inst", None, "tp"),
            P("inst", None, "tp"),
            P("inst", None, "tp"),
            P("inst", None, "tp"),
            P("inst"),
            P(),
        ),
        out_specs=(P("inst", "tp"), P("inst", None, "tp")),
        check_vma=False,
    )
```

time: 262 us -> 52.7 us (0.20)
  waiting for transfers between devices: 122 us -> 0 us
  matrix products: 76 us -> 0 us
  Pallas kernels: 0 us -> 48.2 us
  other arithmetic: 22.8 us -> 0 us
  local copies, waits for them, and re-layouts: 23.3 us -> 3.61 us
  between operations: 14.8 us -> 0.64 us
    all_gather x2 -> x0, waiting for transfers between devices: 121 us -> none  [the longest x1 66.3 us: per_device(): values = lax.all_gather(prompt_value_rows, 'inst', axis=0, tiled=True)]
    dot_general x38 -> x0, matrix products: 76 us -> none  [the longest x16 40.4 us: update(): jnp.einsum('hylj,jhx->hylx', attention_weights.astype(jnp.bfloat16), valu...]
    pallas_call x0 -> x1, Pallas kernels: none -> 48.2 us  [per_device(): pl.pallas_call(kernel, out_shape=(jax.ShapeDtypeStruct((TOK, HEADS * HDIM...]
    reduce_sum x18 -> x0, other arithmetic: 17.6 us -> none  [the longest x16 16.2 us: update(): total = total * factor + jnp.sum(attention_weights, -1)]
    cond x80 -> x0, local copies, waits for them, and re-layouts: 16.3 us -> none
  transfers between devices with their start and end apart: 2 -> 0, of which waited for: 2 -> 0; matrix products, arithmetic and copies ran while one was open for 3% -> 0% of each run, Pallas kernels for 0% -> 0%
where the time goes in v1:
time: 52.7 us; the launch traced here: 52.5 us
  Pallas kernels  48.2 us (91%)
  local copies, waits for them, and re-layouts  3.61 us (7%)
  between operations  0.64 us (1%)
    pallas_call x1, Pallas kernels, per_device(): pl.pallas_call(kernel, out_shape=(jax.ShapeDtypeStruct((TOK, HEADS * HDIM...  48.2 us
    unnamed x2, local copies, waits for them, and re-layouts  3.61 us

profile of v1, /device:TPU:252, one launch (start us, length us, event | category | flops | bytes accessed | tf_op | source)
XLA Modules:
  0.0 52.5 jit_solution(540247148460460261)
XLA Ops:
  0.6 48.2 %shard_map.113 = (bf16[256,1024]{1,0:T(8,128)(2,1)}, bf16[32,4,1024]{2,1,0:T(4,128)(2,1)}) custom-call(bf16[256,1024]{1,0:T(8,128)(2,1)} %q_hbm.1, bf16[256,128]{1,0:T(8,128)(2,1)} %k_hbm.1, bf16[256,128]{1,0:T(8,128)(2,1)} %v_hbm.1, bf16[32,4,1024]{2,1,0:T(4,128)(2,1)} %dq_hbm.1, bf16[32,4,128]{2,1,0:T(4,128)(2,1)} %nk_hbm.1, bf16[32,4,128]{2,1,0:T(4,128)(2,1)} %nv_hbm.1, ...), custom_call_target="tpu_custom_call" | custom-call | tf_op jit(solution)/shard_map/pallas_call | solution.py:342
  48.9 1.9 %copy.14 = bf16[256,1024]{1,0:T(8,128)(2,1)} copy(bf16[256,1024]{1,0:T(8,128)(2,1)} %get-tuple-element.4) | data formatting | bytes 1048576
  50.7 1.7 %copy.15 = bf16[32,4,1024]{2,1,0:T(4,128)(2,1)} copy(bf16[32,4,1024]{2,1,0:T(4,128)(2,1)} %get-tuple-element.5) | data formatting | bytes 524288

commit v2 on v1

--- a/solution.py
+++ b/solution.py
@@ -19,7 +19,7 @@
 STEPS = 4
 NZ = 8
 NINST = 32
-CELL = 4 * TOK
+CHIP = 2 * TOK
 NEG = -1e30
 FACTOR = HDIM**-0.5 * math.log2(math.e)
 
@@ -39,26 +39,22 @@
 ROUTE["B", -4, 0] = "side"
 ROUTE["B", 4, 1] = "side"
 
-EVENTS_NEAR = [("A", -1, 0), ("A", 1, 0), ("A", -1, 1), ("A", 1, 1)]
-EVENTS_SIDE = [("B", 0, 0), ("B", 0, 1)]
-EVENTS_OWN = [
-    ("B", 1, 0),
-    ("A", -2, 0),
-    ("A", 2, 0),
-    ("A", -2, 1),
-    ("A", 2, 1),
-    ("B", -1, 1),
+HEAD = [
+    ([], 'dec'),
+    ([('A', 1, 0), ('A', -1, 0), ('A', -1, 1), ('A', 1, 1)], 'own'),
+    ([('B', 0, 1), ('B', 0, 0)], 'dec'),
 ]
-EVENTS_LOOP = [
-    [("B", -1, 0), ("B", 1, 1)],
-    [("B", 2, 0), ("B", -2, 1)],
-    [("A", -3, 0), ("A", 3, 1), ("A", -3, 1), ("A", 3, 0)],
-    [("B", -2, 0), ("B", 2, 1)],
-    [("B", 3, 0), ("B", -3, 1), ("A", -4, 0), ("A", 4, 1)],
-    [("B", -3, 0), ("B", 3, 1)],
-    [("B", -4, 0), ("B", 4, 1)],
+PLAN = [
+    ([('A', 2, 0), ('A', 2, 1), ('A', -2, 1), ('A', -2, 0)], [('A', -1)]),
+    ([('B', 1, 1), ('B', -1, 1), ('B', -1, 0)], [('A', 2), ('A', 1)]),
+    ([('A', -3, 1), ('B', 2, 0), ('B', 1, 0), ('A', 3, 0), ('A', 3, 1), ('A', -3, 0)], [('B', 0), ('B', -1)]),
+    ([('B', -2, 1), ('B', -2, 0)], [('B', 1), ('A', -3)]),
+    ([('B', 2, 1), ('A', -4, 0), ('A', 4, 1), ('B', -3, 1), ('B', -3, 0)], [('B', -2), ('A', -2)]),
+    ([], [('B', -3), ('B', 2)]),
+    ([('B', -4, 0), ('B', 4, 1), ('B', 3, 1), ('B', 3, 0)], [('A', 3), ('A', 4)]),
+    ([], [('B', 3), ('B', 4)]),
 ]
-CELL_ORDER = (-1, 1, -2, 2, -3, 3, 4)
+TAIL = []
 
 
 def forwards(item):
@@ -70,20 +66,20 @@
         to.append("down")
     if col == "A" and ROUTE.get(("B", d, part)) == "side":
         to.append("side")
-    to.append("twin")
     return to
 
 
 OWN = [("A", 0, 0), ("A", 0, 1)]
 SENDS = [(item, to) for item in OWN + list(ROUTE) for to in forwards(item)]
+CHIPS = [(col, d) for col in ("A", "B") for d in (-3, -2, -1, 0, 1, 2, 3, 4)]
 SEND_INDEX = {key: i for i, key in enumerate(SENDS)}
 
 
 def kernel(
     q_hbm, k_hbm, v_hbm, dq_hbm, nk_hbm, nv_hbm, ck_hbm, cv_hbm, clen_ref, pair_ref,
-    o_hbm, do_hbm,
-    kv, q, dq, nk, nv, ck, cv, qs, acc, top, vd, dqf, dqs, dacc, dtop, nkf, nvf, out, dout,
-    send_sem, recv_sem, local_sem, cache_sem,
+    out, dout,
+    kv, q, dq, nk, nv, ck, cv, qs, acc, top, vd, dqf, dqs, dacc, dtop, nkf, nvf,
+    send_sem, recv_sem, twin_send, twin_recv, local_sem, cache_sem,
 ):
     me = lax.axis_index("inst")
     core = lax.rem(me, 2)
@@ -114,6 +110,19 @@
             device_id_type=MESH,
         )
 
+    def twin(col, d):
+        place = slot(col, d)
+        return pltpu.make_async_remote_copy(
+            src_ref=kv.at[place],
+            dst_ref=kv.at[place],
+            send_sem=twin_send.at[CHIPS.index((col, d))],
+            recv_sem=twin_recv.at[place],
+            device_id={"inst": device["twin"]},
+            device_id_type=MESH,
+        )
+
+    half = set()
+
     def arrived(place, part):
         pltpu.make_async_remote_copy(
             src_ref=kv.at[place, part],
@@ -129,12 +138,21 @@
             arrived(slot(item[0], item[1]), item[2])
             for to in forwards(item):
                 remote(item, to).start()
-
-    def twin_cell(zz):
-        for yy in (0, 1):
-            place = 4 * zz + 2 * yy + 1 - core
-            arrived(place, 0)
-            arrived(place, 1)
+            chip = (item[0], abs(item[1]) if abs(item[1]) == 4 else item[1])
+            if chip in half:
+                twin(*chip).start()
+            half.add(chip)
+
+    def twin_chip(col, d):
+        place = slot(col, d) + 1 - 2 * core
+        pltpu.make_async_remote_copy(
+            src_ref=kv.at[place],
+            dst_ref=kv.at[place],
+            send_sem=twin_send.at[0],
+            recv_sem=twin_recv.at[place],
+            device_id={"inst": device["twin"]},
+            device_id_type=MESH,
+        ).wait_recv()
 
     own = [
         pltpu.make_async_copy(k_hbm, kv.at[me, 0], local_sem.at[0]),
@@ -170,6 +188,7 @@
         own[part].wait()
         for to in forwards(OWN[part]):
             remote(OWN[part], to).start()
+    twin("A", 0).start()
 
     for copy in small:
         copy.wait()
@@ -179,7 +198,7 @@
     for a in range(ROWS):
         nkf[a * STEPS : (a + 1) * STEPS, :] = nk[a].astype(F32)
         nvf[a * STEPS : (a + 1) * STEPS, :] = nv[a].astype(F32)
-    vd[:, HDIM:] = jnp.ones((CELL, HDIM), BF16)
+    vd[:, HDIM:] = jnp.ones((2 * CHIP, HDIM), BF16)
 
     def dot_t(a, b):
         return lax.dot_general(a, b, (((1,), (1,)), ((), ())), preferred_element_type=F32)
@@ -208,92 +227,93 @@
         decode_rows(g)
         return 0
 
-    lax.fori_loop(0, 2, decode_pair, 0)
-    events(EVENTS_NEAR)
-    lax.fori_loop(2, 4, decode_pair, 0)
-    events(EVENTS_SIDE)
-
-    queries.wait()
-    for h in range(HEADS):
-        qs[h] = q[:, h * HDIM : (h + 1) * HDIM]
-    twin_cell(z)
-
-    def cell_keys(zz):
-        return kv[pl.ds(4 * zz, 4), 0].reshape(CELL, HDIM)
-
-    def load_values(zz):
-        vd[:, :HDIM] = kv[pl.ds(4 * zz, 4), 1].reshape(CELL, HDIM)
-
-    load_values(z)
-
-    def first_cell(half):
-        for u in range(HEADS // 2):
-            h = half * (HEADS // 2) + u
-            scores = dot_t(qs[h], cell_keys(z)) * FACTOR
+    def chip_keys(chip):
+        return kv[pl.ds(2 * chip, 2), 0].reshape(CHIP, HDIM)
+
+    def load_values(chip, at):
+        vd[at * CHIP : (at + 1) * CHIP, :HDIM] = kv[pl.ds(2 * chip, 2), 1].reshape(CHIP, HDIM)
+
+    def own_chip():
+        queries.wait()
+        for h in range(HEADS):
+            qs[h] = q[:, h * HDIM : (h + 1) * HDIM]
+        twin_chip("A", 0)
+        chip = me // 2
+        load_values(chip, 0)
+        for h in range(HEADS):
+            scores = dot_t(qs[h], chip_keys(chip))
             key = lax.broadcasted_iota(jnp.int32, scores.shape, 1)
             row = lax.broadcasted_iota(jnp.int32, scores.shape, 0)
-            scores = jnp.where(key <= row + TOK * lax.rem(me, 4), scores, NEG)
-            peak = jnp.max(scores, axis=1, keepdims=True)
-            p = jnp.exp2(scores - peak).astype(BF16)
+            scores = jnp.where(key <= row + TOK * core, scores, NEG)
+            peak = jnp.max(scores, axis=1, keepdims=True) * FACTOR
+            p = jnp.exp2(scores * FACTOR - peak).astype(BF16)
             top[h] = jnp.broadcast_to(peak, (TOK, HDIM))
-            acc[h] = jnp.dot(p, vd[...], preferred_element_type=F32)
-
-    def first_half(half, _):
-        first_cell(half)
-
-        @pl.when(half == 0)
-        def _():
-            events(EVENTS_OWN)
-
-        return 0
-
-    lax.fori_loop(0, 2, first_half, 0)
+            acc[h] = jnp.dot(p, vd[:CHIP], preferred_element_type=F32)
+
+    done = 0
+    for items, what in HEAD:
+        events(items)
+        if what == "dec":
+            lax.fori_loop(done, done + 2, decode_pair, 0)
+            done += 2
+        else:
+            own_chip()
 
     def merge(scores, values, top_ref, acc_ref, index):
         before = top_ref[index]
-        peak = jnp.maximum(before, jnp.max(scores, axis=1, keepdims=True))
+        peak = jnp.maximum(before, jnp.max(scores, axis=1, keepdims=True) * FACTOR)
         top_ref[index] = peak
-        p = jnp.exp2(scores - wide(peak, scores.shape[1])).astype(BF16)
+        p = jnp.exp2(scores * FACTOR - wide(peak, scores.shape[1])).astype(BF16)
         scale = jnp.exp2(before - peak)
         return wide(scale, 2 * HDIM) * acc_ref[index] + jnp.dot(
             p, values, preferred_element_type=F32
         )
 
-    def cell_step(t, _):
-        half = lax.rem(t, 2)
-        j = t // 2
-        for i, items in enumerate(EVENTS_LOOP):
+    def chip_of(col, d):
+        return 2 * lax.rem(z + d + NZ, NZ) + (y if col == "A" else 1 - y)
+
+    def step(t, _):
+        for i, (items, chips) in enumerate(PLAN):
 
             @pl.when(t == i)
-            def _(items=items):
+            def _(items=items, chips=chips):
                 events(items)
-
-        away = j // 2 + 1
-        zz = lax.rem(z + NZ + jnp.where(lax.rem(j, 2) == 0, -away, away), NZ)
-
-        @pl.when(half == 0)
+                for chip in chips:
+                    twin_chip(*chip)
+
+        left = chip_of(*PLAN[0][1][0])
+        right = chip_of(*PLAN[0][1][-1])
+        paired = len(PLAN[0][1]) - 1
+        for i, (_, chips) in enumerate(PLAN[1:], 1):
+            left = jnp.where(t == i, chip_of(*chips[0]), left)
+            right = jnp.where(t == i, chip_of(*chips[-1]), right)
+            paired = jnp.where(t == i, len(chips) - 1, paired)
+        mine = me // 2
+        left_seen = left < mine
+        right_seen = jnp.logical_and(right < mine, paired == 1)
+
+        @pl.when(jnp.logical_and(left_seen, right_seen))
         def _():
-            twin_cell(zz)
-
-        @pl.when(zz < z)
+            load_values(left, 0)
+            load_values(right, 1)
+            for h in range(HEADS):
+                keys = jnp.concatenate([chip_keys(left), chip_keys(right)], axis=0)
+                acc[h] = merge(dot_t(qs[h], keys), vd[...], top, acc, h)
+
+        @pl.when(jnp.logical_xor(left_seen, right_seen))
         def _():
-            @pl.when(half == 0)
-            def _():
-                load_values(zz)
-
-            for u in range(HEADS // 2):
-                h = half * (HEADS // 2) + u
-                scores = dot_t(qs[h], cell_keys(zz)) * FACTOR
-                acc[h] = merge(scores, vd[...], top, acc, h)
+            only = jnp.where(left_seen, left, right)
+            load_values(only, 0)
+            for h in range(HEADS):
+                acc[h] = merge(dot_t(qs[h], chip_keys(only)), vd[:CHIP], top, acc, h)
 
         return 0
 
-    lax.fori_loop(0, 14, cell_step, 0)
+    lax.fori_loop(0, len(PLAN), step, 0)
+    events(TAIL)
 
     for h in range(HEADS):
         out[:, h * HDIM : (h + 1) * HDIM] = (acc[h, :, :HDIM] / acc[h, :, HDIM:]).astype(BF16)
-    out_copy = pltpu.make_async_copy(out, o_hbm, local_sem.at[6])
-    out_copy.start()
 
     pair = pair_ref[me]
     new_keys = ROWS * STEPS
@@ -326,27 +346,26 @@
     lax.fori_loop(0, 4, decode_last, 0)
     for h in range(HEADS):
         dout[:, :, h * HDIM : (h + 1) * HDIM] = dqf[:, pl.ds(h, STEPS, stride=HEADS), :].astype(BF16)
-    dout_copy = pltpu.make_async_copy(dout, do_hbm, local_sem.at[7])
-    dout_copy.start()
     for item, to in SENDS:
         remote(item, to).wait_send()
-    out_copy.wait()
-    dout_copy.wait()
+    for chip in CHIPS:
+        twin(*chip).wait_send()
 
 
 def per_device(*args):
     any_spec = pl.BlockSpec(memory_space=pl.ANY)
     smem = pl.BlockSpec(memory_space=pltpu.SMEM)
     vmem = pltpu.VMEM
+    vspec = pl.BlockSpec(memory_space=pltpu.VMEM)
     per = STEPS * HEADS
     return pl.pallas_call(
         kernel,
         out_shape=(
-            jax.ShapeDtypeStruct((TOK, HEADS * HDIM), BF16),
-            jax.ShapeDtypeStruct((ROWS, STEPS, HEADS * HDIM), BF16),
+            pltpu.VMEM((TOK, HEADS * HDIM), BF16),
+            pltpu.VMEM((ROWS, STEPS, HEADS * HDIM), BF16),
         ),
         in_specs=[any_spec] * 8 + [smem, smem],
-        out_specs=(any_spec, any_spec),
+        out_specs=(vspec, vspec),
         scratch_shapes=[
             vmem((NINST, 2, TOK, HDIM), BF16),
             vmem((TOK, HEADS * HDIM), BF16),
@@ -358,17 +377,17 @@
             vmem((HEADS, TOK, HDIM), BF16),
             vmem((HEADS, TOK, 2 * HDIM), F32),
             vmem((HEADS, TOK, HDIM), F32),
-            vmem((CELL, 2 * HDIM), BF16),
+            vmem((2 * CHIP, 2 * HDIM), BF16),
             vmem((ROWS, per, HDIM), F32),
             vmem((ROWS, per, HDIM), BF16),
             vmem((ROWS, per, 2 * HDIM), F32),
             vmem((ROWS, per, HDIM), F32),
             vmem((ROWS * STEPS, HDIM), F32),
             vmem((ROWS * STEPS, HDIM), F32),
-            vmem((TOK, HEADS * HDIM), BF16),
-            vmem((ROWS, STEPS, HEADS * HDIM), BF16),
             pltpu.SemaphoreType.DMA((len(SENDS),)),
             pltpu.SemaphoreType.DMA((NINST, 2)),
+            pltpu.SemaphoreType.DMA((len(CHIPS),)),
+            pltpu.SemaphoreType.DMA((NINST,)),
             pltpu.SemaphoreType.DMA((8,)),
             pltpu.SemaphoreType.DMA((4, 2)),
         ],

time: 52.7 us -> 42.2 us (0.80)
  Pallas kernels: 48.2 us -> 40 us
  local copies, waits for them, and re-layouts: 3.61 us -> 1.5 us
    pallas_call x1, Pallas kernels: 48.2 us -> 40 us  [per_device(): pl.pallas_call(kernel, out_shape=(pltpu.VMEM((TOK, HEADS * HDIM), BF16),...]
    unnamed x2, local copies, waits for them, and re-layouts: 3.61 us -> 1.5 us
where the time goes in v2:
time: 42.2 us; the launch traced here: 42.1 us
  Pallas kernels  40 us (95%)
  local copies, waits for them, and re-layouts  1.5 us (4%)
  between operations  0.64 us (2%)
    pallas_call x1, Pallas kernels, per_device(): pl.pallas_call(kernel, out_shape=(pltpu.VMEM((TOK, HEADS * HDIM), BF16),...  40 us
    unnamed x2, local copies, waits for them, and re-layouts  1.5 us

profile of v2, /device:TPU:252, one launch (start us, length us, event | category | flops | bytes accessed | tf_op | source)
XLA Modules:
  0.0 42.1 jit_solution(87228916449318105)
XLA Ops:
  0.6 40.0 %shard_map.113 = (bf16[256,1024]{1,0:T(8,128)(2,1)S(1)}, bf16[32,4,1024]{2,1,0:T(4,128)(2,1)S(1)}) custom-call(bf16[256,1024]{1,0:T(8,128)(2,1)} %q_hbm.1, bf16[256,128]{1,0:T(8,128)(2,1)} %k_hbm.1, bf16[256,128]{1,0:T(8,128)(2,1)} %v_hbm.1, bf16[32,4,1024]{2,1,0:T(4,128)(2,1)} %dq_hbm.1, bf16[32,4,128]{2,1,0:T(4,128)(2,1)} %nk_hbm.1, ...), custom_call_target="tpu_custom_call" | custom-call | tf_op jit(solution)/shard_map/pallas_call | solution.py:361
  40.6 0.8 %copy.14 = bf16[256,1024]{1,0:T(8,128)(2,1)} copy(bf16[256,1024]{1,0:T(8,128)(2,1)S(1)} %get-tuple-element.2) | data formatting | bytes 1048576
  41.4 0.7 %copy.15 = bf16[32,4,1024]{2,1,0:T(4,128)(2,1)} copy(bf16[32,4,1024]{2,1,0:T(4,128)(2,1)S(1)} %get-tuple-element.3) | data formatting | bytes 524288

commit v3 on v2

--- a/solution.py
+++ b/solution.py
@@ -23,21 +23,38 @@
 NEG = -1e30
 FACTOR = HDIM**-0.5 * math.log2(math.e)
 
-ROUTE = {}
-for _d in (1, 2, 3):
-    for _part in (0, 1):
-        ROUTE["A", -_d, _part] = "down"
-        ROUTE["A", _d, _part] = "up"
-    ROUTE["B", -_d, 0] = "down"
-    ROUTE["B", _d, 1] = "up"
-    ROUTE["B", _d, 0] = "side"
-    ROUTE["B", -_d, 1] = "side"
-ROUTE["A", -4, 0] = "down"
-ROUTE["A", 4, 1] = "up"
-ROUTE["B", 0, 0] = "side"
-ROUTE["B", 0, 1] = "side"
-ROUTE["B", -4, 0] = "side"
-ROUTE["B", 4, 1] = "side"
+ROUTE = {
+    ('A', -1, 0): (1, 0),
+    ('A', 1, 0): (-1, 0),
+    ('A', -1, 1): (1, 0),
+    ('A', 1, 1): (-1, 0),
+    ('B', -1, 0): (1, 0),
+    ('B', 1, 1): (-1, 0),
+    ('B', 1, 0): (0, 1),
+    ('B', -1, 1): (0, 1),
+    ('A', -2, 0): (1, 0),
+    ('A', 2, 0): (-1, 0),
+    ('A', -2, 1): (1, 0),
+    ('A', 2, 1): (-1, 0),
+    ('B', -2, 0): (1, 0),
+    ('B', 2, 1): (-1, 0),
+    ('B', 2, 0): (0, 1),
+    ('B', -2, 1): (0, 1),
+    ('A', -3, 0): (1, 0),
+    ('A', 3, 0): (-1, 0),
+    ('A', -3, 1): (1, 0),
+    ('A', 3, 1): (-1, 0),
+    ('B', -3, 0): (1, 0),
+    ('B', 3, 1): (-1, 0),
+    ('B', 3, 0): (0, 1),
+    ('B', -3, 1): (0, 1),
+    ('A', -4, 0): (1, 0),
+    ('A', 4, 1): (-1, 0),
+    ('B', 0, 0): (0, 1),
+    ('B', 0, 1): (0, 1),
+    ('B', -4, 0): (0, 1),
+    ('B', 4, 1): (0, 1),
+}
 
 HEAD = [
     ([], 'dec'),
@@ -59,26 +76,25 @@
 
 def forwards(item):
     col, d, part = item
-    to = []
-    if ROUTE.get((col, d - 1, part)) == "down":
-        to.append("up")
-    if ROUTE.get((col, d + 1, part)) == "up":
-        to.append("down")
-    if col == "A" and ROUTE.get(("B", d, part)) == "side":
-        to.append("side")
-    return to
+    moves = []
+    for (to_col, to_d, to_part), (dz, dy) in ROUTE.items():
+        from_col = to_col if dy == 0 else "AB"["BA".index(to_col)]
+        if (from_col, to_d + dz, to_part) == (col, d, part):
+            moves.append((abs(to_d), dz, dy))
+    return [(dz, dy) for _, dz, dy in sorted(moves)]
 
 
 OWN = [("A", 0, 0), ("A", 0, 1)]
 SENDS = [(item, to) for item in OWN + list(ROUTE) for to in forwards(item)]
 CHIPS = [(col, d) for col in ("A", "B") for d in (-3, -2, -1, 0, 1, 2, 3, 4)]
+PARTNERS = sorted({((way * dz) % NZ, dy) for dz, dy in ROUTE.values() for way in (1, -1)})
 SEND_INDEX = {key: i for i, key in enumerate(SENDS)}
 
 
 def kernel(
     q_hbm, k_hbm, v_hbm, dq_hbm, nk_hbm, nv_hbm, ck_hbm, cv_hbm, clen_ref, pair_ref,
     out, dout,
-    kv, q, dq, nk, nv, ck, cv, qs, acc, top, vd, dqf, dqs, dacc, dtop, nkf, nvf,
+    kv, q, dq, nk, nv, ck, cv, qs, acc, top, vd, even, odd, dqf, dqs, dacc, dtop, nkf, nvf,
     send_sem, recv_sem, twin_send, twin_recv, local_sem, cache_sem,
 ):
     me = lax.axis_index("inst")
@@ -91,12 +107,10 @@
         yy = y if col == "A" else 1 - y
         return 4 * zz + 2 * yy + core
 
-    device = {
-        "up": 4 * lax.rem(z + 1, NZ) + 2 * y + core,
-        "down": 4 * lax.rem(z + NZ - 1, NZ) + 2 * y + core,
-        "side": 4 * z + 2 * (1 - y) + core,
-        "twin": 4 * z + 2 * y + 1 - core,
-    }
+    def device(dz, dy):
+        return {"inst": 4 * lax.rem(z + dz + NZ, NZ) + 2 * (y if dy == 0 else 1 - y) + core}
+
+    twin_device = {"inst": me + 1 - 2 * core}
 
     def remote(item, to):
         col, d, part = item
@@ -106,7 +120,7 @@
             dst_ref=kv.at[place, part],
             send_sem=send_sem.at[SEND_INDEX[item, to]],
             recv_sem=recv_sem.at[place, part],
-            device_id={"inst": device[to]},
+            device_id=device(*to),
             device_id_type=MESH,
         )
 
@@ -117,7 +131,7 @@
             dst_ref=kv.at[place],
             send_sem=twin_send.at[CHIPS.index((col, d))],
             recv_sem=twin_recv.at[place],
-            device_id={"inst": device["twin"]},
+            device_id=twin_device,
             device_id_type=MESH,
         )
 
@@ -129,7 +143,7 @@
             dst_ref=kv.at[place, part],
             send_sem=send_sem.at[0],
             recv_sem=recv_sem.at[place, part],
-            device_id={"inst": device["twin"]},
+            device_id=twin_device,
             device_id_type=MESH,
         ).wait_recv()
 
@@ -150,7 +164,7 @@
             dst_ref=kv.at[place],
             send_sem=twin_send.at[0],
             recv_sem=twin_recv.at[place],
-            device_id={"inst": device["twin"]},
+            device_id=twin_device,
             device_id_type=MESH,
         ).wait_recv()
 
@@ -180,9 +194,10 @@
     queries.start()
 
     barrier = pltpu.get_barrier_semaphore()
-    for to in ("up", "down", "side", "twin"):
-        pl.semaphore_signal(barrier, inc=1, device_id={"inst": device[to]}, device_id_type=MESH)
-    pl.semaphore_wait(barrier, 4)
+    for to in PARTNERS:
+        pl.semaphore_signal(barrier, inc=1, device_id=device(*to), device_id_type=MESH)
+    pl.semaphore_signal(barrier, inc=1, device_id=twin_device, device_id_type=MESH)
+    pl.semaphore_wait(barrier, len(PARTNERS) + 1)
 
     for part in (0, 1):
         own[part].wait()
@@ -198,7 +213,7 @@
     for a in range(ROWS):
         nkf[a * STEPS : (a + 1) * STEPS, :] = nk[a].astype(F32)
         nvf[a * STEPS : (a + 1) * STEPS, :] = nv[a].astype(F32)
-    vd[:, HDIM:] = jnp.ones((2 * CHIP, HDIM), BF16)
+    vd[:, HDIM:] = jnp.ones((4 * CHIP, HDIM), BF16)
 
     def dot_t(a, b):
         return lax.dot_general(a, b, (((1,), (1,)), ((), ())), preferred_element_type=F32)
@@ -209,10 +224,11 @@
     ones = jnp.ones((CACHE, HDIM), BF16)
 
     def decode_rows(g):
-        for copy in cache_copies(g):
-            copy.wait()
-        for u in range(8):
-            a = 8 * g + u
+        for part in (0, 1):
+            for copy in cache_copies(2 * g + part):
+                copy.wait()
+        for u in range(16):
+            a = 16 * g + u
             scores = dot_t(dqs[a], ck[a]) * FACTOR
             live = lax.broadcasted_iota(jnp.int32, scores.shape, 1) < clen_ref[a]
             scores = jnp.where(live, scores, NEG)
@@ -222,10 +238,6 @@
             dacc[a] = jnp.dot(
                 p, jnp.concatenate([cv[a], ones], axis=1), preferred_element_type=F32
             )
-
-    def decode_pair(g, _):
-        decode_rows(g)
-        return 0
 
     def chip_keys(chip):
         return kv[pl.ds(2 * chip, 2), 0].reshape(CHIP, HDIM)
@@ -254,8 +266,8 @@
     for items, what in HEAD:
         events(items)
         if what == "dec":
-            lax.fori_loop(done, done + 2, decode_pair, 0)
-            done += 2
+            decode_rows(done)
+            done += 1
         else:
             own_chip()
 
@@ -281,31 +293,58 @@
                 for chip in chips:
                     twin_chip(*chip)
 
-        left = chip_of(*PLAN[0][1][0])
-        right = chip_of(*PLAN[0][1][-1])
-        paired = len(PLAN[0][1]) - 1
-        for i, (_, chips) in enumerate(PLAN[1:], 1):
-            left = jnp.where(t == i, chip_of(*chips[0]), left)
-            right = jnp.where(t == i, chip_of(*chips[-1]), right)
-            paired = jnp.where(t == i, len(chips) - 1, paired)
         mine = me // 2
-        left_seen = left < mine
-        right_seen = jnp.logical_and(right < mine, paired == 1)
-
-        @pl.when(jnp.logical_and(left_seen, right_seen))
+        chips = []
+        seen = []
+        for k in range(max(len(c) for _, c in PLAN)):
+            chip = mine
+            for i, (_, listed) in enumerate(PLAN):
+                if k < len(listed):
+                    chip = jnp.where(t == i, chip_of(*listed[k]), chip)
+            chips.append(chip)
+            seen.append(chip < mine)
+        for last in range(len(chips) - 1, 0, -1):
+            for k in range(last):
+                swap = jnp.logical_and(jnp.logical_not(seen[k]), seen[k + 1])
+                chips[k], chips[k + 1] = (
+                    jnp.where(swap, chips[k + 1], chips[k]),
+                    jnp.where(swap, chips[k], chips[k + 1]),
+                )
+                seen[k], seen[k + 1] = (
+                    jnp.logical_or(seen[k], seen[k + 1]),
+                    jnp.logical_and(seen[k], seen[k + 1]),
+                )
+        count = sum(flag.astype(jnp.int32) for flag in seen)
+
+        def attend(some):
+            width = len(some) * CHIP
+            for k, chip in enumerate(some):
+                load_values(chip, k)
+
+            def score(h):
+                keys = jnp.concatenate([chip_keys(chip) for chip in some], axis=0)
+                (even if h % 2 == 0 else odd)[:, :width] = dot_t(qs[h], keys)
+
+            score(0)
+            for h in range(HEADS):
+                if h + 1 < HEADS:
+                    score(h + 1)
+                scores = (even if h % 2 == 0 else odd)[:, :width]
+                acc[h] = merge(scores, vd[:width], top, acc, h)
+
+        if len(chips) > 3:
+
+            @pl.when(count == 4)
+            def _():
+                attend(chips[:4])
+
+        @pl.when(jnp.logical_or(count == 2, count == 3))
         def _():
-            load_values(left, 0)
-            load_values(right, 1)
-            for h in range(HEADS):
-                keys = jnp.concatenate([chip_keys(left), chip_keys(right)], axis=0)
-                acc[h] = merge(dot_t(qs[h], keys), vd[...], top, acc, h)
-
-        @pl.when(jnp.logical_xor(left_seen, right_seen))
+            attend(chips[:2])
+
+        @pl.when(jnp.logical_or(count == 1, count == 3))
         def _():
-            only = jnp.where(left_seen, left, right)
-            load_values(only, 0)
-            for h in range(HEADS):
-                acc[h] = merge(dot_t(qs[h], chip_keys(only)), vd[:CHIP], top, acc, h)
+            attend([jnp.where(count == 3, chips[min(2, len(chips) - 1)], chips[0])])
 
         return 0
 
@@ -323,16 +362,19 @@
     values = vd[: TOK + new_keys, :]
     per = STEPS * HEADS
 
-    def decode_last(g, _):
-        rows = pl.ds(8 * g, 8)
-        size = 8 * per
-        scores = dot_t(dqs[rows].reshape(size, HDIM), keys) * FACTOR
-        column = lax.broadcasted_iota(jnp.int32, (size, new_keys), 1)
-        row = lax.broadcasted_iota(jnp.int32, (size, new_keys), 0) + g * size
-        keep = jnp.logical_and(
-            column // STEPS == row // per,
-            lax.rem(column, STEPS) <= lax.rem(row // HEADS, STEPS),
-        )
+    size = 8 * per
+    column = lax.broadcasted_iota(jnp.int32, (size, new_keys), 1)
+    row = lax.broadcasted_iota(jnp.int32, (size, new_keys), 0)
+    allowed = (column & (STEPS - 1)) <= ((row >> 3) & (STEPS - 1))
+    behind = (column >> 2) - (row >> 5)
+
+    def last_scores(g):
+        return dot_t(dqs[8 * g : 8 * g + 8].reshape(size, HDIM), keys)
+
+    def decode_last(g, scores):
+        rows = slice(8 * g, 8 * g + 8)
+        keep = jnp.logical_and(allowed, behind == 8 * g)
+        scores = scores * FACTOR
         fresh = jnp.where(keep, scores[:, TOK:], NEG)
         scores = jnp.concatenate([scores[:, :TOK], fresh], axis=1)
         before = dtop[rows].reshape(size, HDIM)
@@ -341,9 +383,9 @@
         total = wide(jnp.exp2(before - peak), 2 * HDIM) * dacc[rows].reshape(size, 2 * HDIM)
         total = total + jnp.dot(p, values, preferred_element_type=F32)
         dqf[rows] = (total[:, :HDIM] / total[:, HDIM:]).reshape(8, per, HDIM)
-        return 0
-
-    lax.fori_loop(0, 4, decode_last, 0)
+
+    for g in range(ROWS // 8):
+        decode_last(g, last_scores(g))
     for h in range(HEADS):
         dout[:, :, h * HDIM : (h + 1) * HDIM] = dqf[:, pl.ds(h, STEPS, stride=HEADS), :].astype(BF16)
     for item, to in SENDS:
@@ -377,7 +419,9 @@
             vmem((HEADS, TOK, HDIM), BF16),
             vmem((HEADS, TOK, 2 * HDIM), F32),
             vmem((HEADS, TOK, HDIM), F32),
-            vmem((2 * CHIP, 2 * HDIM), BF16),
+            vmem((4 * CHIP, 2 * HDIM), BF16),
+            vmem((TOK, 4 * CHIP), F32),
+            vmem((TOK, 4 * CHIP), F32),
             vmem((ROWS, per, HDIM), F32),
             vmem((ROWS, per, HDIM), BF16),
             vmem((ROWS, per, 2 * HDIM), F32),

time: 42.2 us -> 39.9 us (0.945)
  Pallas kernels: 40 us -> 37.6 us
    pallas_call x1, Pallas kernels: 40 us -> 37.6 us  [per_device(): pl.pallas_call(kernel, out_shape=(pltpu.VMEM((TOK, HEADS * HDIM), BF16),...]
where the time goes in v3:
time: 39.9 us; the launch traced here: 39.8 us
  Pallas kernels  37.6 us (94%)
  local copies, waits for them, and re-layouts  1.5 us (4%)
  between operations  0.64 us (2%)
    pallas_call x1, Pallas kernels, per_device(): pl.pallas_call(kernel, out_shape=(pltpu.VMEM((TOK, HEADS * HDIM), BF16),...  37.6 us
    unnamed x2, local copies, waits for them, and re-layouts  1.5 us

profile of v3, /device:TPU:252, one launch (start us, length us, event | category | flops | bytes accessed | tf_op | source)
XLA Modules:
  0.0 39.8 jit_solution(2689158390818025570)
XLA Ops:
  0.6 37.6 %shard_map.113 = (bf16[256,1024]{1,0:T(8,128)(2,1)S(1)}, bf16[32,4,1024]{2,1,0:T(4,128)(2,1)S(1)}) custom-call(bf16[256,1024]{1,0:T(8,128)(2,1)} %q_hbm.1, bf16[256,128]{1,0:T(8,128)(2,1)} %k_hbm.1, bf16[256,128]{1,0:T(8,128)(2,1)} %v_hbm.1, bf16[32,4,1024]{2,1,0:T(4,128)(2,1)} %dq_hbm.1, bf16[32,4,128]{2,1,0:T(4,128)(2,1)} %nk_hbm.1, ...), custom_call_target="tpu_custom_call" | custom-call | tf_op jit(solution)/shard_map/pallas_call | solution.py:403
  38.3 0.8 %copy.14 = bf16[256,1024]{1,0:T(8,128)(2,1)} copy(bf16[256,1024]{1,0:T(8,128)(2,1)S(1)} %get-tuple-element.2) | data formatting | bytes 1048576
  39.1 0.7 %copy.15 = bf16[32,4,1024]{2,1,0:T(4,128)(2,1)} copy(bf16[32,4,1024]{2,1,0:T(4,128)(2,1)S(1)} %get-tuple-element.3) | data formatting | bytes 524288

commit v4 on v3

--- a/solution.py
+++ b/solution.py
@@ -213,7 +213,7 @@
     for a in range(ROWS):
         nkf[a * STEPS : (a + 1) * STEPS, :] = nk[a].astype(F32)
         nvf[a * STEPS : (a + 1) * STEPS, :] = nv[a].astype(F32)
-    vd[:, HDIM:] = jnp.ones((4 * CHIP, HDIM), BF16)
+    vd[:, HDIM:] = jnp.ones((2 * CHIP, HDIM), BF16)
 
     def dot_t(a, b):
         return lax.dot_general(a, b, (((1,), (1,)), ((), ())), preferred_element_type=F32)
@@ -252,8 +252,15 @@
         twin_chip("A", 0)
         chip = me // 2
         load_values(chip, 0)
+
+        def own_scores(h):
+            (even if h % 2 == 0 else odd)[:, :CHIP] = dot_t(qs[h], chip_keys(chip))
+
+        own_scores(0)
         for h in range(HEADS):
-            scores = dot_t(qs[h], chip_keys(chip))
+            if h + 1 < HEADS:
+                own_scores(h + 1)
+            scores = (even if h % 2 == 0 else odd)[:, :CHIP]
             key = lax.broadcasted_iota(jnp.int32, scores.shape, 1)
             row = lax.broadcasted_iota(jnp.int32, scores.shape, 0)
             scores = jnp.where(key <= row + TOK * core, scores, NEG)
@@ -384,8 +391,12 @@
         total = total + jnp.dot(p, values, preferred_element_type=F32)
         dqf[rows] = (total[:, :HDIM] / total[:, HDIM:]).reshape(8, per, HDIM)
 
+    width = TOK + new_keys
+    even[:, :width] = last_scores(0)
     for g in range(ROWS // 8):
-        decode_last(g, last_scores(g))
+        if g + 1 < ROWS // 8:
+            (odd if g % 2 == 0 else even)[:, :width] = last_scores(g + 1)
+        decode_last(g, (even if g % 2 == 0 else odd)[:, :width])
     for h in range(HEADS):
         dout[:, :, h * HDIM : (h + 1) * HDIM] = dqf[:, pl.ds(h, STEPS, stride=HEADS), :].astype(BF16)
     for item, to in SENDS:
@@ -419,9 +430,9 @@
             vmem((HEADS, TOK, HDIM), BF16),
             vmem((HEADS, TOK, 2 * HDIM), F32),
             vmem((HEADS, TOK, HDIM), F32),
-            vmem((4 * CHIP, 2 * HDIM), BF16),
-            vmem((TOK, 4 * CHIP), F32),
-            vmem((TOK, 4 * CHIP), F32),
+            vmem((2 * CHIP, 2 * HDIM), BF16),
+            vmem((TOK, 2 * CHIP), F32),
+            vmem((TOK, 2 * CHIP), F32),
             vmem((ROWS, per, HDIM), F32),
             vmem((ROWS, per, HDIM), BF16),
             vmem((ROWS, per, 2 * HDIM), F32),

time: 39.9 us -> 39.8 us (level)
  no operation moved by 1% of the time
where the time goes in v4:
time: 39.8 us; the launch traced here: 39.7 us
  Pallas kernels  37.5 us (94%)
  local copies, waits for them, and re-layouts  1.5 us (4%)
  between operations  0.64 us (2%)
    pallas_call x1, Pallas kernels, per_device(): pl.pallas_call(kernel, out_shape=(pltpu.VMEM((TOK, HEADS * HDIM), BF16),...  37.5 us
    unnamed x2, local copies, waits for them, and re-layouts  1.5 us

profile of v4, /device:TPU:252, one launch (start us, length us, event | category | flops | bytes accessed | tf_op | source)
XLA Modules:
  0.0 39.7 jit_solution(12275787756842455733)
XLA Ops:
  0.6 37.5 %shard_map.113 = (bf16[256,1024]{1,0:T(8,128)(2,1)S(1)}, bf16[32,4,1024]{2,1,0:T(4,128)(2,1)S(1)}) custom-call(bf16[256,1024]{1,0:T(8,128)(2,1)} %q_hbm.1, bf16[256,128]{1,0:T(8,128)(2,1)} %k_hbm.1, bf16[256,128]{1,0:T(8,128)(2,1)} %v_hbm.1, bf16[32,4,1024]{2,1,0:T(4,128)(2,1)} %dq_hbm.1, bf16[32,4,128]{2,1,0:T(4,128)(2,1)} %nk_hbm.1, ...), custom_call_target="tpu_custom_call" | custom-call | tf_op jit(solution)/shard_map/pallas_call | solution.py:414
  38.2 0.8 %copy.14 = bf16[256,1024]{1,0:T(8,128)(2,1)} copy(bf16[256,1024]{1,0:T(8,128)(2,1)S(1)} %get-tuple-element.2) | data formatting | bytes 1048576
  39.0 0.7 %copy.15 = bf16[32,4,1024]{2,1,0:T(4,128)(2,1)} copy(bf16[32,4,1024]{2,1,0:T(4,128)(2,1)S(1)} %get-tuple-element.3) | data formatting | bytes 524288

commit v5 on v4

--- a/solution.py
+++ b/solution.py
@@ -197,6 +197,7 @@
     for to in PARTNERS:
         pl.semaphore_signal(barrier, inc=1, device_id=device(*to), device_id_type=MESH)
     pl.semaphore_signal(barrier, inc=1, device_id=twin_device, device_id_type=MESH)
+    vd[:, HDIM:] = jnp.ones((2 * CHIP, HDIM), BF16)
     pl.semaphore_wait(barrier, len(PARTNERS) + 1)
 
     for part in (0, 1):
@@ -213,7 +214,6 @@
     for a in range(ROWS):
         nkf[a * STEPS : (a + 1) * STEPS, :] = nk[a].astype(F32)
         nvf[a * STEPS : (a + 1) * STEPS, :] = nv[a].astype(F32)
-    vd[:, HDIM:] = jnp.ones((2 * CHIP, HDIM), BF16)
 
     def dot_t(a, b):
         return lax.dot_general(a, b, (((1,), (1,)), ((), ())), preferred_element_type=F32)

time: 39.8 us -> 39.8 us (level)
  no operation moved by 1% of the time
where the time goes in v5:
time: 39.8 us; the launch traced here: 39.7 us
  Pallas kernels  37.5 us (94%)
  local copies, waits for them, and re-layouts  1.5 us (4%)
  between operations  0.64 us (2%)
    pallas_call x1, Pallas kernels, per_device(): pl.pallas_call(kernel, out_shape=(pltpu.VMEM((TOK, HEADS * HDIM), BF16),...  37.5 us
    unnamed x2, local copies, waits for them, and re-layouts  1.5 us

profile of v5, /device:TPU:252, one launch (start us, length us, event | category | flops | bytes accessed | tf_op | source)
XLA Modules:
  0.0 39.7 jit_solution(4229343332321240425)
XLA Ops:
  0.6 37.5 %shard_map.113 = (bf16[256,1024]{1,0:T(8,128)(2,1)S(1)}, bf16[32,4,1024]{2,1,0:T(4,128)(2,1)S(1)}) custom-call(bf16[256,1024]{1,0:T(8,128)(2,1)} %q_hbm.1, bf16[256,128]{1,0:T(8,128)(2,1)} %k_hbm.1, bf16[256,128]{1,0:T(8,128)(2,1)} %v_hbm.1, bf16[32,4,1024]{2,1,0:T(4,128)(2,1)} %dq_hbm.1, bf16[32,4,128]{2,1,0:T(4,128)(2,1)} %nk_hbm.1, ...), custom_call_target="tpu_custom_call" | custom-call | tf_op jit(solution)/shard_map/pallas_call | solution.py:414
  38.2 0.8 %copy.14 = bf16[256,1024]{1,0:T(8,128)(2,1)} copy(bf16[256,1024]{1,0:T(8,128)(2,1)S(1)} %get-tuple-element.2) | data formatting | bytes 1048576
  39.0 0.7 %copy.15 = bf16[32,4,1024]{2,1,0:T(4,128)(2,1)} copy(bf16[32,4,1024]{2,1,0:T(4,128)(2,1)S(1)} %get-tuple-element.3) | data formatting | bytes 524288
